TPU v7x, 512 devices: a whole 4x4x16 slice. The times are simulated.
512 devices in a mesh: pipe: 8 (over y, core), expert: 64 (over z, x).
Axes of the slice: x: 4, y: 4, z: 16, core: 2. Of those that a mesh axis runs over, the one named last changes fastest.
Arguments:
- upstream: bfloat16 [8, 4096, 2048], P('pipe', 'expert'), may hold values from -6 to 6
- expert_ids: int32 [8, 4096, 8], P('pipe', 'expert'), may hold values from 0 to 63, all different within a row; in each aligned block of 64 rows (0 to 63, 64 to 127, ..., all dimensions but the last counted through in order) at most 16 rows name the same one
- gate_weights: bfloat16 [8, 4096, 8], P('pipe', 'expert'), may hold values from 0.099609375 to 2
- expert_weight: bfloat16 [8, 64, 768, 2048], P('pipe', 'expert'), may hold values from -0.125 to 0.125
Outputs:
- hidden_grad: bfloat16 [8, 4096, 8, 768], P('pipe', 'expert')
Inputs may be any that keep to these rules, and one draw needn't show every extreme that they name: `expert_ids`: each token names 8 different experts. Among the 64 tokens of one device (aligned blocks of the section's tokens) no expert is named by more than 16 tokens, and in some blocks one expert is named by exactly 16.
All inputs are finite; a program needn't handle non-finite values.
Results may differ from a plain program's by a relative error of at most 0.001.
Values may be sent and summed in bfloat16 or wider, within the bound.
A program may use at most 64 MiB of HBM per device.

v0:
```python
import jax
import jax.numpy as jnp
from jax import lax
from jax.sharding import PartitionSpec as P


def shifted(block, axis, distance):
    devices = range(lax.axis_size(axis))
    route = [((i - distance) % len(devices), i) for i in devices]
    return lax.ppermute(block, axis, route)


def per_device(upstream, expert_ids, gate_weights, expert_weight):
    section_grad = shifted(upstream, "pipe", -1)[0]
    route_ids = expert_ids[0]
    route_gates = gate_weights[0]
    weight_mat = expert_weight[0, 0]
    token_count, top_count = route_ids.shape
    owner_count = lax.axis_size("expert")
    capacity = 2 * token_count * top_count // owner_count
    owners = jnp.arange(owner_count, dtype=jnp.int32)
    slot_index = jnp.arange(capacity, dtype=jnp.int32)
    matched = (route_ids[:, :, None] == owners[None, None, :]).astype(jnp.int32)
    hit_count = jnp.sum(matched, axis=1)
    slot_rank = jnp.cumsum(hit_count, axis=0) - hit_count
    route_rank = jnp.sum(matched * slot_rank[:, None, :], axis=2)
    position = route_ids * capacity + route_rank
    gate_owner = jnp.einsum(
        "tk,tke->te", route_gates.astype(jnp.float32), matched.astype(jnp.float32)
    )
    slot_pick = (hit_count[:, :, None] == 1) & (slot_rank[:, :, None] == slot_index[None, None, :])
    send_rows = jnp.einsum(
        "tem,td->emd",
        slot_pick.astype(jnp.bfloat16),
        section_grad,
        preferred_element_type=jnp.float32,
    ).astype(jnp.bfloat16)
    send_gates = jnp.einsum("tem,te->em", slot_pick.astype(jnp.float32), gate_owner).astype(
        jnp.bfloat16
    )
    got_rows, got_gates = (
        lax.all_to_all(send_rows, "expert", split_axis=0, concat_axis=0, tiled=True),
        lax.all_to_all(send_gates, "expert", split_axis=0, concat_axis=0, tiled=True),
    )
    blocks = got_rows.shape[0]
    slot_span = got_rows.shape[1]
    flat_rows = got_rows.reshape(blocks * slot_span, got_rows.shape[2])
    product = lax.dot_general(
        flat_rows, weight_mat, (((1,), (1,)), ((), ())), preferred_element_type=jnp.float32
    )
    product = product.reshape(blocks, slot_span, weight_mat.shape[0])
    returned = lax.all_to_all(
        (product * got_gates.astype(jnp.float32)[:, :, None]).astype(jnp.bfloat16),
        "expert",
        split_axis=0,
        concat_axis=0,
        tiled=True,
    )
    flat_back = returned.reshape(owner_count * capacity, returned.shape[2])
    hidden_grad = jnp.take(flat_back, position.reshape(token_count * top_count), axis=0)
    return hidden_grad.reshape(token_count, top_count, returned.shape[2])[None]


def solution(mesh):
    in_specs = (
        P("pipe", "expert", None),
        P("pipe", "expert", None),
        P("pipe", "expert", None),
        P("pipe", "expert", None, None),
    )
    out_specs = P("pipe", "expert", None, None)
    return jax.shard_map(
        per_device, mesh=mesh, in_specs=in_specs, out_specs=out_specs, check_vma=False
    )
```

profile of v0, /device:TPU:24, one launch (start us, length us, event | category | flops | bytes accessed | tf_op | source)
XLA Modules:
  0.0 331.5 jit_solution(3555599838181836220)
XLA Ops:
  0.0 0.0 copy-start
  0.0 0.2 collective-permute-start
  0.2 0.9 copy.29
  1.1 0.2 convert_reduce_fusion
  1.3 0.1 copy.32
  1.4 0.1 reduce_window_sum.11
  1.5 0.1 copy.33
  1.6 0.8 copy.36
  2.4 0.9 fusion.7
  3.2 0.8 copy.44
  4.1 0.8 select_reduce_fusion
  4.9 0.8 copy.43
  5.7 0.7 copy.34
  6.4 18.6 %all-to-all-start.1 = ((bf16[64,1,16]{2,1,0:T(2,128)(2,1)}), bf16[64,1,16]{2,1,0:T(2,128)(2,1)S(1)}, u32[]{:S(2)}, u32[]{:S(2)}) async-start(bf16[64,1,16]{2,1,0:T(2,128)(2,1)} %copy.34), calls=%async_computation.1 | async-start | bytes 65536 | tf_op jit(solution)/shard_map/all_to_all | solution.py:43
  25.0 0.0 collective-permute-done
  25.0 3.2 convolution_convert_fusion
  28.2 11.5 %all-to-all-done.1 = bf16[64,1,16]{2,1,0:T(2,128)(2,1)S(1)} async-done(((bf16[64,1,16]{2,1,0:T(2,128)(2,1)}), bf16[64,1,16]{2,1,0:T(2,128)(2,1)S(1)}, u32[]{:S(2)}, u32[]{:S(2)}) %all-to-all-start.1) | async-done | bytes 2080 | tf_op jit(solution)/shard_map/all_to_all | solution.py:43
  39.7 5.7 %all-to-all-start = ((bf16[64,16,2048]{2,1,0:T(8,128)(2,1)}), bf16[64,16,2048]{2,1,0:T(8,128)(2,1)}, u32[]{:S(2)}, u32[]{:S(2)}) async-start(bf16[64,16,2048]{2,1,0:T(8,128)(2,1)} %convolution_convert_fusion), calls=%async_computation | async-start | bytes 8388608 | tf_op jit(solution)/shard_map/all_to_all | solution.py:42
  45.4 189.2 %all-to-all-done = bf16[64,16,2048]{2,1,0:T(8,128)(2,1)} async-done(((bf16[64,16,2048]{2,1,0:T(8,128)(2,1)}), bf16[64,16,2048]{2,1,0:T(8,128)(2,1)}, u32[]{:S(2)}, u32[]{:S(2)}) %all-to-all-start) | async-done | bytes 4194336 | tf_op jit(solution)/shard_map/all_to_all | solution.py:42
  234.6 0.0 copy-done
  234.6 6.8 %multiply_convert_fusion = bf16[64,16,768]{2,1,0:T(8,128)(2,1)} fusion(bf16[64,16,2048]{2,1,0:T(8,128)(2,1)} %all-to-all-done, bf16[1,1,768,2048]{3,2,1,0:T(8,128)(2,1)S(1)} %copy-done, f32[64,16]{1,0:T(8,128)S(1)} %bitcast.34), kind=kOutput, calls=%fused_computation.4 | convolution fusion | flops 3222798336 | bytes 8916992 | tf_op jit(solution)/shard_map/dot_general | solution.py:48
  241.4 0.0 copy-start.1
  241.4 6.2 %all-to-all-start.2 = ((bf16[64,16,768]{2,1,0:T(8,128)(2,1)}), bf16[64,16,768]{2,1,0:T(8,128)(2,1)}, u32[]{:S(2)}, u32[]{:S(2)}) async-start(bf16[64,16,768]{2,1,0:T(8,128)(2,1)} %multiply_convert_fusion), calls=%async_computation.2 | async-start | bytes 3145728 | tf_op jit(solution)/shard_map/all_to_all | solution.py:52
  247.7 1.2 select_reduce_fusion.1
  248.9 0.1 reduce_sum.22
  249.0 0.1 copy.30
  249.1 0.0 copy-done.1
  249.1 0.1 copy.35
  249.1 0.1 mul.48
  249.3 0.1 copy.31
  249.4 75.2 %all-to-all-done.2 = bf16[64,16,768]{2,1,0:T(8,128)(2,1)} async-done(((bf16[64,16,768]{2,1,0:T(8,128)(2,1)}), bf16[64,16,768]{2,1,0:T(8,128)(2,1)}, u32[]{:S(2)}, u32[]{:S(2)}) %all-to-all-start.2) | async-done | bytes 1572896 | tf_op jit(solution)/shard_map/all_to_all | solution.py:52
  324.6 4.7 %gather_fusion = bf16[512,768]{1,0:T(8,128)(2,1)} fusion(bf16[1024,768]{1,0:T(8,128)(2,1)} %bitcast.14, s32[1024]{0:T(1024)S(1)} %pad_clamp_fusion), kind=kCustom, calls=%fused_computation | custom fusion | bytes 1574912 | tf_op jit(solution)/shard_map/jit(_take)/gather | solution.py:60
  329.3 2.2 bitcast_select_fusion
  (7 shorter events, 0.1 us)
Async XLA Ops:
  0.0 234.6 %copy-start = (bf16[1,1,768,2048]{3,2,1,0:T(8,128)(2,1)S(1)}, bf16[1,1,768,2048]{3,2,1,0:T(8,128)(2,1)}, u32[]{:S(2)}) copy-start(bf16[1,1,768,2048]{3,2,1,0:T(8,128)(2,1)} %param.7) | copy-start | bytes 9437188
  0.0 25.0 %collective-permute-start = (bf16[1,64,2048]{2,1,0:T(8,128)(2,1)}, bf16[1,64,2048]{2,1,0:T(8,128)(2,1)S(1)}, u32[]{:S(2)}, u32[]{:S(2)}) collective-permute-start(bf16[1,64,2048]{2,1,0:T(8,128)(2,1)} %param.4), channel_id=1, source_target_pairs={{64,0},{128,64},{192,128},{256,192},{320,256},{384,320},{448,384},... | collective-permute-start | bytes 786440 | tf_op jit(solution)/shard_map/ppermute | solution.py:10
  6.4 33.2 %all-to-all-start.1 = ((bf16[64,1,16]{2,1,0:T(2,128)(2,1)}), bf16[64,1,16]{2,1,0:T(2,128)(2,1)S(1)}, u32[]{:S(2)}, u32[]{:S(2)}) async-start(bf16[64,1,16]{2,1,0:T(2,128)(2,1)} %copy.34), calls=%async_computation.1 | async-start | bytes 65536 | tf_op jit(solution)/shard_map/all_to_all | solution.py:43
  39.7 194.9 %all-to-all-start = ((bf16[64,16,2048]{2,1,0:T(8,128)(2,1)}), bf16[64,16,2048]{2,1,0:T(8,128)(2,1)}, u32[]{:S(2)}, u32[]{:S(2)}) async-start(bf16[64,16,2048]{2,1,0:T(8,128)(2,1)} %convolution_convert_fusion), calls=%async_computation | async-start | bytes 8388608 | tf_op jit(solution)/shard_map/all_to_all | solution.py:42
  241.4 7.6 %copy-start.1 = (s32[1,64,8]{1,2,0:T(8,128)S(1)}, s32[1,64,8]{1,2,0:T(8,128)}, u32[]{:S(2)}) copy-start(s32[1,64,8]{1,2,0:T(8,128)} %param.5) | copy-start | bytes 6148
  241.4 83.2 %all-to-all-start.2 = ((bf16[64,16,768]{2,1,0:T(8,128)(2,1)}), bf16[64,16,768]{2,1,0:T(8,128)(2,1)}, u32[]{:S(2)}, u32[]{:S(2)}) async-start(bf16[64,16,768]{2,1,0:T(8,128)(2,1)} %multiply_convert_fusion), calls=%async_computation.2 | async-start | bytes 3145728 | tf_op jit(solution)/shard_map/all_to_all | solution.py:52
where the time goes:
time: 332 us; the launch traced here: 331 us
  waiting for transfers between devices  276 us (83%)
  starting transfers between devices  30.6 us (9%)
  matrix products  10.9 us (3%)
  local copies, waits for them, and re-layouts  9.39 us (3%)
  other arithmetic  4.57 us (1%)
    all_to_all x1, waiting for transfers between devices, per_device(): lax.all_to_all(send_rows, 'expert', split_axis=0, concat_axis=0, tiled=True)  189 us
    all_to_all x1, waiting for transfers between devices, per_device(): lax.all_to_all((product * got_gates.astype(jnp.float32)[:, :, None]).asty...  75.2 us
    all_to_all x1, starting transfers between devices, per_device(): lax.all_to_all(send_gates, 'expert', split_axis=0, concat_axis=0, tiled=T...  18.6 us
    all_to_all x1, waiting for transfers between devices, per_device(): lax.all_to_all(send_gates, 'expert', split_axis=0, concat_axis=0, tiled=T...  11.5 us
    dot_general x1, matrix products, per_device(): lax.dot_general(flat_rows, weight_mat, (((1,), (1,)), ((), ())), preferre...  6.81 us
  transfers between devices with their start and end apart: 4, of which 3 were waited for; matrix products, arithmetic and copies ran while one was open for 3% of the time, Pallas kernels for 0%

commit v1 on v0

v1 whole, which is shorter than its diff:
```python
import functools

import jax
import jax.numpy as jnp
from jax import lax
from jax.experimental import pallas as pl
from jax.experimental.pallas import tpu as pltpu
from jax.sharding import PartitionSpec as P

MESH = pl.DeviceIdType.MESH
NX = 4
MOST = 16
LANES = 128
HALF = 64


def iota(shape, dim):
    return lax.broadcasted_iota(jnp.int32, shape, dim)


def kernel(
    pipes,
    experts,
    up_ref,
    ids_ref,
    gates_ref,
    w_hbm,
    out_ref,
    tok,
    table,
    own_table,
    sel,
    rows_in,
    prod,
    ret,
    acc,
    pos,
    w_ref,
    local_sem,
    ring_send,
    ring_recv,
    table_send,
    table_recv,
    shift_sem,
    sel_send,
    sel_recv,
    ret_send,
    ret_recv,
):
    nz = experts // NX
    steps = nz // 2
    tokens, width = up_ref.shape
    topk = ids_ref.shape[0]
    hidden = w_hbm.shape[0]
    p = lax.axis_index("pipe")
    e = lax.axis_index("expert")
    z = e // NX
    x = e % NX
    after = (p + 1) % pipes
    before = (p + pipes - 1) % pipes

    def at(zz, xx):
        return ((zz + nz) % nz) * NX + xx

    barrier = pltpu.get_barrier_semaphore()

    def greet(d, carry):
        pl.semaphore_signal(barrier, inc=1, device_id=(p, (e + d) % experts), device_id_type=MESH)
        return carry

    lax.fori_loop(1, experts, greet, 0)
    for xx in range(NX):
        pl.semaphore_signal(barrier, inc=1, device_id=(after, at(z, xx)), device_id_type=MESH)
    pl.semaphore_signal(barrier, inc=1, device_id=(before, e), device_id_type=MESH)
    pl.semaphore_wait(barrier, experts - 1 + NX + 1)

    def ring(direction, hop, src):
        dst = hop if direction == 0 else nz - hop
        return pltpu.make_async_remote_copy(
            src_ref=src,
            dst_ref=tok.at[dst],
            send_sem=ring_send.at[direction, hop],
            recv_sem=ring_recv.at[direction, hop],
            device_id=(p, at(z + 1 - 2 * direction, x)),
            device_id_type=MESH,
        )

    def ring_table(direction, hop, src):
        dst = hop if direction == 0 else nz - hop
        return pltpu.make_async_remote_copy(
            src_ref=src,
            dst_ref=table.at[dst],
            send_sem=table_send.at[direction, hop],
            recv_sem=table_recv.at[direction, hop],
            device_id=(p, at(z + 1 - 2 * direction, x)),
            device_id_type=MESH,
        )

    ring(0, 1, up_ref).start()
    ring(1, 1, up_ref).start()
    own_copy = pltpu.make_async_copy(up_ref, tok.at[0], local_sem.at[0])
    own_copy.start()
    w_copy = pltpu.make_async_copy(w_hbm, w_ref, local_sem.at[1])
    w_copy.start()

    packed = jnp.concatenate(
        [ids_ref[...].astype(jnp.float32), gates_ref[...].astype(jnp.float32)], axis=0
    ).astype(jnp.bfloat16)
    eye = (iota((tokens, tokens), 0) == iota((tokens, tokens), 1)).astype(jnp.bfloat16)
    columns = lax.dot_general(
        eye, packed, (((1,), (1,)), ((), ())), preferred_element_type=jnp.float32
    )
    lane = iota((tokens, LANES), 1)
    lane_expert = (lane % HALF).astype(jnp.float32)
    named = jnp.zeros((tokens, LANES), jnp.float32)
    gate = jnp.zeros((tokens, LANES), jnp.float32)
    for k in range(topk):
        hit = columns[:, k : k + 1] == lane_expert
        named = jnp.where(hit, 1.0, named)
        gate = jnp.where(hit, columns[:, topk + k : topk + k + 1], gate)
    lower = (iota((tokens, tokens), 1) < iota((tokens, tokens), 0)).astype(jnp.bfloat16)
    rank = jnp.dot(lower, named.astype(jnp.bfloat16), preferred_element_type=jnp.float32)
    value = jnp.where(lane < HALF, (iota((tokens, LANES), 0) + 1).astype(jnp.float32), gate)
    value = jnp.where(named > 0.5, value, 0.0)
    table_rows = [
        jnp.sum(jnp.where(rank == float(r), value, 0.0), axis=0, keepdims=True)
        for r in range(MOST)
    ]
    own_table[...] = jnp.concatenate(table_rows, axis=0).astype(jnp.bfloat16)

    shift = pltpu.make_async_remote_copy(
        src_ref=own_table,
        dst_ref=table.at[0],
        send_sem=shift_sem.at[0],
        recv_sem=shift_sem.at[1],
        device_id=(after, e),
        device_id_type=MESH,
    )
    shift.start()

    ranks = []
    for k in range(topk):
        hit = (columns[:, k : k + 1] == lane_expert) & (lane < HALF)
        ranks.append(jnp.sum(jnp.where(hit, rank, 0.0), axis=1, keepdims=True))
    lane8 = iota((tokens, 2 * topk), 1)
    both = jnp.where(lane8 < topk, columns, 0.0)
    for k in range(topk):
        both = jnp.where(lane8 == topk + k, ranks[k], both)
    routes = tokens * topk
    spread = (iota((routes, tokens), 0) // topk == iota((routes, tokens), 1)).astype(jnp.bfloat16)
    by_route = jnp.dot(spread, both.astype(jnp.bfloat16), preferred_element_type=jnp.float32)
    which = iota((routes, 2 * topk), 0) % topk
    lane_r = iota((routes, 2 * topk), 1)
    slot = jnp.sum(
        jnp.where(lane_r == which, by_route * MOST, 0.0)
        + jnp.where(lane_r == which + topk, by_route, 0.0),
        axis=1,
        keepdims=True,
    )
    slot = slot - (z * (NX * MOST)).astype(jnp.float32)
    slot = jnp.where(slot < 0.0, slot + float(experts * MOST), slot)
    pos[...] = jnp.broadcast_to(slot, (routes, LANES))

    shift.wait()
    ring_table(0, 1, table.at[0]).start()
    ring_table(1, 1, table.at[0]).start()
    w_copy.wait()

    def pair(i):
        return i % steps, nz - i

    def sel_copy(i, xx):
        return pltpu.make_async_remote_copy(
            src_ref=sel.at[i - 1, xx],
            dst_ref=rows_in.at[i - 1, x],
            send_sem=sel_send.at[i - 1, xx],
            recv_sem=sel_recv.at[i - 1, x],
            device_id=(before, at(z, xx)),
            device_id_type=MESH,
        )

    def choose(i):
        table_lane = iota((MOST, LANES), 1)
        token_lane = (iota((MOST, tokens), 1) + 1).astype(jnp.float32)
        for half, j in enumerate(pair(i)):
            slots = table[j].astype(jnp.float32)
            picks = []
            for xx in range(NX):
                expert = at(z, xx)
                token = jnp.sum(
                    jnp.where(table_lane == expert, slots, 0.0), axis=1, keepdims=True
                )
                weight = jnp.sum(
                    jnp.where(table_lane == expert + HALF, slots, 0.0), axis=1, keepdims=True
                )
                picks.append((token == token_lane).astype(jnp.bfloat16))
                sel[i - 1, xx, half * MOST : (half + 1) * MOST, width:] = jnp.broadcast_to(
                    weight, (MOST, LANES)
                ).astype(jnp.bfloat16)
            pick = jnp.concatenate(picks, axis=0)
            part = min(512, width)
            for c in range(0, width, part):
                rows = jnp.dot(
                    pick, tok[j, :, c : c + part], preferred_element_type=jnp.float32
                ).astype(jnp.bfloat16)
                for xx in range(NX):
                    sel[i - 1, xx, half * MOST : (half + 1) * MOST, c : c + part] = rows[
                        xx * MOST : (xx + 1) * MOST
                    ]
        for d in range(NX):
            sel_copy(i, (x + d) % NX).start()

    def ret_copy(i, half, j, d, local=False):
        xx = (x + d) % NX
        src = prod.at[i - 1, pl.ds(pl.multiple_of((xx * 2 + half) * MOST, MOST), MOST)]
        dst = ret.at[j, pl.ds(pl.multiple_of(x * MOST, MOST), MOST)]
        if local:
            return pltpu.make_async_copy(src, dst, ret_recv.at[j, x])
        return pltpu.make_async_remote_copy(
            src_ref=src,
            dst_ref=dst,
            send_sem=ret_send.at[i - 1, half, d],
            recv_sem=ret_recv.at[j, x],
            device_id=(p, at(z - j, xx)),
            device_id_type=MESH,
        )

    def multiply(i):
        for d in range(NX):
            xx = (x + d) % NX
            pltpu.make_async_copy(
                rows_in.at[i - 1, xx], rows_in.at[i - 1, xx], sel_recv.at[i - 1, xx]
            ).wait()
        count = NX * 2 * MOST
        gates = rows_in[i - 1, :, :, width:].reshape(count, LANES).astype(jnp.float32)
        for n in range(0, hidden, 256):
            out = lax.dot_general(
                rows_in[i - 1, :, :, :width].reshape(count, width),
                w_ref[n : n + 256],
                (((1,), (1,)), ((), ())),
                preferred_element_type=jnp.float32,
            )
            for c in range(0, 256, LANES):
                prod[i - 1, :, n + c : n + c + LANES] = (
                    out[:, c : c + LANES] * gates
                ).astype(jnp.bfloat16)
        for half, j in enumerate(pair(i)):
            for d in range(NX):
                if half == 0 and d == 0:
                    pl.when(i == steps)(lambda: ret_copy(i, 0, j, 0, local=True).start())
                    pl.when(i < steps)(lambda: ret_copy(i, 0, j, 0).start())
                else:
                    ret_copy(i, half, j, d).start()

    def step(i, carry):
        @pl.when(i < steps)
        def _():
            ring(0, i, up_ref).wait_recv()

        @pl.when(i < steps - 1)
        def _():
            ring(0, i + 1, tok.at[i]).start()

        ring(1, i, up_ref).wait_recv()

        @pl.when(i < steps)
        def _():
            ring(1, i + 1, tok.at[nz - i]).start()
            ring_table(0, i, table.at[0]).wait_recv()

        @pl.when(i < steps - 1)
        def _():
            ring_table(0, i + 1, table.at[i]).start()

        ring_table(1, i, table.at[0]).wait_recv()

        @pl.when(i < steps)
        def _():
            ring_table(1, i + 1, table.at[nz - i]).start()

        @pl.when(i == steps)
        def _():
            own_copy.wait()

        choose(i)

        @pl.when(i >= 2)
        def _():
            multiply(i - 1)

        return carry

    lax.fori_loop(1, steps + 1, step, 0)
    multiply(steps)
    acc[...] = jnp.zeros_like(acc)

    def place(i, carry):
        a, b = pair(i)
        for j in (a, b):
            for xx in range(NX):
                here = ret.at[j, xx * MOST : (xx + 1) * MOST]
                pltpu.make_async_copy(here, here, ret_recv.at[j, xx]).wait()
        span = NX * MOST
        part = min(128, routes)
        lane_q = iota((part, 2 * span), 1)
        want = jnp.where(lane_q < span, a * span + lane_q, (b - 1) * span + lane_q).astype(
            jnp.float32
        )
        rows = jnp.concatenate([ret[a], ret[b]], axis=0)
        for r in range(0, routes, part):
            pick = (pos[r : r + part, : 2 * span] == want).astype(jnp.bfloat16)
            for n in range(0, hidden, 256):
                acc[r : r + part, n : n + 256] += jnp.dot(
                    pick, rows[:, n : n + 256], preferred_element_type=jnp.float32
                )
        return carry

    lax.fori_loop(1, steps + 1, place, 0)
    out_ref[...] = acc[...].astype(jnp.bfloat16)

    def drain(i, carry):
        @pl.when(i < steps)
        def _():
            ring(0, i, up_ref).wait_send()
            ring_table(0, i, table.at[0]).wait_send()

        ring(1, i, up_ref).wait_send()
        ring_table(1, i, table.at[0]).wait_send()
        for xx in range(NX):
            sel_copy(i, xx).wait_send()
        for half, j in enumerate(pair(i)):
            for d in range(NX):
                if half == 0 and d == 0:
                    pl.when(i < steps)(lambda: ret_copy(i, 0, j, 0).wait_send())
                else:
                    ret_copy(i, half, j, d).wait_send()
        return carry

    lax.fori_loop(1, steps + 1, drain, 0)


def per_device(pipes, experts, upstream, expert_ids, gate_weights, expert_weight):
    _, tokens, width = upstream.shape
    topk = expert_ids.shape[2]
    hidden = expert_weight.shape[2]
    nz = experts // NX
    steps = nz // 2
    routes = tokens * topk
    dma = pltpu.SemaphoreType.DMA
    out = pl.pallas_call(
        functools.partial(kernel, pipes, experts),
        out_shape=jax.ShapeDtypeStruct((routes, hidden), jnp.bfloat16),
        in_specs=[
            pl.BlockSpec(memory_space=pl.ANY),
            pl.BlockSpec(memory_space=pltpu.VMEM),
            pl.BlockSpec(memory_space=pltpu.VMEM),
            pl.BlockSpec(memory_space=pl.ANY),
        ],
        out_specs=pl.BlockSpec(memory_space=pltpu.VMEM),
        scratch_shapes=[
            pltpu.VMEM((nz, tokens, width), jnp.bfloat16),
            pltpu.VMEM((nz, MOST, LANES), jnp.bfloat16),
            pltpu.VMEM((MOST, LANES), jnp.bfloat16),
            pltpu.VMEM((steps, NX, 2 * MOST, width + LANES), jnp.bfloat16),
            pltpu.VMEM((steps, NX, 2 * MOST, width + LANES), jnp.bfloat16),
            pltpu.VMEM((steps, NX * 2 * MOST, hidden), jnp.bfloat16),
            pltpu.VMEM((nz, NX * MOST, hidden), jnp.bfloat16),
            pltpu.VMEM((routes, hidden), jnp.float32),
            pltpu.VMEM((routes, LANES), jnp.float32),
            pltpu.VMEM((hidden, width), jnp.bfloat16),
            dma((2,)),
            dma((2, steps + 1)),
            dma((2, steps + 1)),
            dma((2, steps + 1)),
            dma((2, steps + 1)),
            dma((2,)),
            dma((steps, NX)),
            dma((steps, NX)),
            dma((steps, 2, NX)),
            dma((nz, NX)),
        ],
        compiler_params=pltpu.CompilerParams(
            collective_id=0, has_side_effects=True, vmem_limit_bytes=48 * 1024 * 1024
        ),
        cost_estimate=pl.CostEstimate(
            flops=2 * 2 * routes * width * hidden, bytes_accessed=8 << 20, transcendentals=0
        ),
    )(
        upstream[0],
        jnp.swapaxes(expert_ids[0], 0, 1),
        jnp.swapaxes(gate_weights[0], 0, 1),
        expert_weight[0, 0],
    )
    return out.reshape(1, tokens, topk, hidden)


def solution(mesh):
    in_specs = (
        P("pipe", "expert", None),
        P("pipe", "expert", None),
        P("pipe", "expert", None),
        P("pipe", "expert", None, None),
    )
    out_specs = P("pipe", "expert", None, None)
    return jax.shard_map(
        functools.partial(per_device, mesh.shape["pipe"], mesh.shape["expert"]),
        mesh=mesh,
        in_specs=in_specs,
        out_specs=out_specs,
        check_vma=False,
    )
```

time: 332 us -> 154 us (0.46)
  the two profiles are of different devices: /device:TPU:24 before, /device:TPU:232 now
where the time goes in v1:
time: 154 us; the launch traced here: 153 us
  Pallas kernels  148 us (96%)
  local copies, waits for them, and re-layouts  5.09 us (3%)
    pallas_call x1, Pallas kernels, per_device(): pl.pallas_call(functools.partial(kernel, pipes, experts), out_shape=jax.S...  148 us
    unnamed x9, local copies, waits for them, and re-layouts  5.09 us

profile of v1, /device:TPU:232, one launch (start us, length us, event | category | flops | bytes accessed | tf_op | source)
XLA Modules:
  0.0 153.5 jit_solution(7024257716921921450)
XLA Ops:
  0.0 0.0 copy-start
  0.0 1.9 %copy-done = bf16[1,1,768,2048]{3,2,1,0:T(8,128)(2,1)S(1)} copy-done((bf16[1,1,768,2048]{3,2,1,0:T(8,128)(2,1)S(1)}, bf16[1,1,768,2048]{3,2,1,0:T(8,128)(2,1)}, u32[]{:S(2)}) %copy-start) | copy-done | bytes 3145752
  1.9 0.0 copy-start.1
  1.9 0.9 copy-done.1
  2.8 0.0 copy-start.2
  2.8 0.7 copy-done.2
  3.5 0.0 copy-start.3
  3.5 0.7 copy-done.3
  4.2 148.4 %shard_map.46 = bf16[512,768]{1,0:T(8,128)(2,1)S(1)} custom-call(bf16[64,2048]{1,0:T(8,128)(2,1)S(1)} %bitcast.11, s32[8,64]{1,0:T(8,128)S(1)} %bitcast.12, bf16[8,64]{1,0:T(8,128)(2,1)S(1)} %bitcast.13, bf16[768,2048]{1,0:T(8,128)(2,1)S(1)} %bitcast.10), custom_call_target="tpu_custom_call" | custom-call | flops 3221225472 | bytes 8388608 | tf_op jit(solution)/shard_map/pallas_call | solution.py:350
  152.6 0.9 copy.6
Async XLA Ops:
  0.0 1.9 %copy-start = (bf16[1,1,768,2048]{3,2,1,0:T(8,128)(2,1)S(1)}, bf16[1,1,768,2048]{3,2,1,0:T(8,128)(2,1)}, u32[]{:S(2)}) copy-start(bf16[1,1,768,2048]{3,2,1,0:T(8,128)(2,1)} %param.7) | copy-start | bytes 9437188
  1.9 0.9 copy-start.1
  2.8 0.7 copy-start.2
  3.5 0.7 copy-start.3

commit v2 on v1

--- a/solution.py
+++ b/solution.py
@@ -12,6 +12,7 @@
 MOST = 16
 LANES = 128
 HALF = 64
+CHUNKS = 2
 
 
 def iota(shape, dim):
@@ -22,8 +23,8 @@
     pipes,
     experts,
     up_ref,
-    ids_ref,
-    gates_ref,
+    ids_hbm,
+    gates_hbm,
     w_hbm,
     out_ref,
     tok,
@@ -36,6 +37,8 @@
     acc,
     pos,
     w_ref,
+    ids_ref,
+    gates_ref,
     local_sem,
     ring_send,
     ring_recv,
@@ -50,7 +53,7 @@
     nz = experts // NX
     steps = nz // 2
     tokens, width = up_ref.shape
-    topk = ids_ref.shape[0]
+    topk = ids_hbm.shape[0]
     hidden = w_hbm.shape[0]
     p = lax.axis_index("pipe")
     e = lax.axis_index("expert")
@@ -62,25 +65,32 @@
     def at(zz, xx):
         return ((zz + nz) % nz) * NX + xx
 
+    ids_copy = pltpu.make_async_copy(ids_hbm, ids_ref, local_sem.at[2])
+    ids_copy.start()
+    gates_copy = pltpu.make_async_copy(gates_hbm, gates_ref, local_sem.at[3])
+    gates_copy.start()
+    own_copy = pltpu.make_async_copy(up_ref, tok.at[0], local_sem.at[0])
+    own_copy.start()
+    w_copy = pltpu.make_async_copy(w_hbm, w_ref, local_sem.at[1])
+    w_copy.start()
+
     barrier = pltpu.get_barrier_semaphore()
 
-    def greet(d, carry):
-        pl.semaphore_signal(barrier, inc=1, device_id=(p, (e + d) % experts), device_id_type=MESH)
-        return carry
-
-    lax.fori_loop(1, experts, greet, 0)
+    for other in (at(z + 1, x), at(z - 1, x)):
+        pl.semaphore_signal(barrier, inc=1, device_id=(p, other), device_id_type=MESH)
     for xx in range(NX):
         pl.semaphore_signal(barrier, inc=1, device_id=(after, at(z, xx)), device_id_type=MESH)
     pl.semaphore_signal(barrier, inc=1, device_id=(before, e), device_id_type=MESH)
-    pl.semaphore_wait(barrier, experts - 1 + NX + 1)
-
-    def ring(direction, hop, src):
+    pl.semaphore_wait(barrier, 2 + NX + 1)
+
+    def ring(direction, hop, src, c):
         dst = hop if direction == 0 else nz - hop
+        part = pl.ds(c * (tokens // CHUNKS), tokens // CHUNKS)
         return pltpu.make_async_remote_copy(
-            src_ref=src,
-            dst_ref=tok.at[dst],
-            send_sem=ring_send.at[direction, hop],
-            recv_sem=ring_recv.at[direction, hop],
+            src_ref=src.at[part],
+            dst_ref=tok.at[dst, part],
+            send_sem=ring_send.at[direction, hop, c],
+            recv_sem=ring_recv.at[direction, hop, c],
             device_id=(p, at(z + 1 - 2 * direction, x)),
             device_id_type=MESH,
         )
@@ -96,12 +106,11 @@
             device_id_type=MESH,
         )
 
-    ring(0, 1, up_ref).start()
-    ring(1, 1, up_ref).start()
-    own_copy = pltpu.make_async_copy(up_ref, tok.at[0], local_sem.at[0])
-    own_copy.start()
-    w_copy = pltpu.make_async_copy(w_hbm, w_ref, local_sem.at[1])
-    w_copy.start()
+    for c in range(CHUNKS):
+        for way in range(2):
+            ring(way, 1, up_ref, c).start()
+    ids_copy.wait()
+    gates_copy.wait()
 
     packed = jnp.concatenate(
         [ids_ref[...].astype(jnp.float32), gates_ref[...].astype(jnp.float32)], axis=0
@@ -253,19 +262,20 @@
                     ret_copy(i, half, j, d).start()
 
     def step(i, carry):
+        for c in range(CHUNKS):
+            for way in range(2):
+                last = steps - 1 + (c * 2 // CHUNKS == way)
+
+                @pl.when(i <= last)
+                def _():
+                    ring(way, i, up_ref, c).wait_recv()
+
+                @pl.when(i < last)
+                def _():
+                    ring(way, i + 1, tok.at[i if way == 0 else nz - i], c).start()
+
         @pl.when(i < steps)
         def _():
-            ring(0, i, up_ref).wait_recv()
-
-        @pl.when(i < steps - 1)
-        def _():
-            ring(0, i + 1, tok.at[i]).start()
-
-        ring(1, i, up_ref).wait_recv()
-
-        @pl.when(i < steps)
-        def _():
-            ring(1, i + 1, tok.at[nz - i]).start()
             ring_table(0, i, table.at[0]).wait_recv()
 
         @pl.when(i < steps - 1)
@@ -319,12 +329,11 @@
     out_ref[...] = acc[...].astype(jnp.bfloat16)
 
     def drain(i, carry):
-        @pl.when(i < steps)
-        def _():
-            ring(0, i, up_ref).wait_send()
-            ring_table(0, i, table.at[0]).wait_send()
-
-        ring(1, i, up_ref).wait_send()
+        for c in range(CHUNKS):
+            for way in range(2):
+                last = steps - 1 + (c * 2 // CHUNKS == way)
+                pl.when(i <= last)(lambda: ring(way, i, up_ref, c).wait_send())
+        pl.when(i < steps)(lambda: ring_table(0, i, table.at[0]).wait_send())
         ring_table(1, i, table.at[0]).wait_send()
         for xx in range(NX):
             sel_copy(i, xx).wait_send()
@@ -351,10 +360,10 @@
         functools.partial(kernel, pipes, experts),
         out_shape=jax.ShapeDtypeStruct((routes, hidden), jnp.bfloat16),
         in_specs=[
-            pl.BlockSpec(memory_space=pl.ANY),
-            pl.BlockSpec(memory_space=pltpu.VMEM),
-            pl.BlockSpec(memory_space=pltpu.VMEM),
-            pl.BlockSpec(memory_space=pl.ANY),
+            pl.BlockSpec(memory_space=pltpu.HBM),
+            pl.BlockSpec(memory_space=pltpu.HBM),
+            pl.BlockSpec(memory_space=pltpu.HBM),
+            pl.BlockSpec(memory_space=pltpu.HBM),
         ],
         out_specs=pl.BlockSpec(memory_space=pltpu.VMEM),
         scratch_shapes=[
@@ -368,9 +377,11 @@
             pltpu.VMEM((routes, hidden), jnp.float32),
             pltpu.VMEM((routes, LANES), jnp.float32),
             pltpu.VMEM((hidden, width), jnp.bfloat16),
-            dma((2,)),
-            dma((2, steps + 1)),
-            dma((2, steps + 1)),
+            pltpu.VMEM((topk, tokens), jnp.int32),
+            pltpu.VMEM((topk, tokens), jnp.bfloat16),
+            dma((4,)),
+            dma((2, steps + 1, CHUNKS)),
+            dma((2, steps + 1, CHUNKS)),
             dma((2, steps + 1)),
             dma((2, steps + 1)),
             dma((2,)),
@@ -380,7 +391,7 @@
             dma((nz, NX)),
         ],
         compiler_params=pltpu.CompilerParams(
-            collective_id=0, has_side_effects=True, vmem_limit_bytes=48 * 1024 * 1024
+            collective_id=0, has_side_effects=True, vmem_limit_bytes=62 * 1024 * 1024
         ),
         cost_estimate=pl.CostEstimate(
             flops=2 * 2 * routes * width * hidden, bytes_accessed=8 << 20, transcendentals=0

time: 154 us -> 144 us (0.935)
  the two profiles are of different devices: /device:TPU:232 before, /device:TPU:8 now
where the time goes in v2:
time: 144 us
  Pallas kernels  142 us (99%)
  local copies, waits for them, and re-layouts  2.06 us (1%)
    pallas_call x1, Pallas kernels, per_device(): pl.pallas_call(functools.partial(kernel, pipes, experts), out_shape=jax.S...  142 us

profile of v2, /device:TPU:8, one launch (start us, length us, event | category | flops | bytes accessed | tf_op | source)
XLA Modules:
  0.0 144.2 jit_solution(14317232497014560569)
XLA Ops:
  0.0 142.1 %shard_map.46 = bf16[512,768]{1,0:T(8,128)(2,1)} custom-call(bf16[64,2048]{1,0:T(8,128)(2,1)} %bitcast.11, s32[8,64]{1,0:T(8,128)} %bitcast.12, bf16[8,64]{1,0:T(8,128)(2,1)} %bitcast.13, bf16[768,2048]{1,0:T(8,128)(2,1)} %bitcast.10), custom_call_target="tpu_custom_call" | custom-call | flops 3221225472 | bytes 8388608 | tf_op jit(solution)/shard_map/pallas_call | solution.py:359
  142.1 2.1 %copy.6 = bf16[1,64,8,768]{3,2,1,0:T(8,128)(2,1)} copy(bf16[1,64,8,768]{3,2,1,0:T(8,128)(2,1)} %bitcast.9) | data formatting | bytes 1572864

commit v3 on v2

--- a/solution.py
+++ b/solution.py
@@ -33,6 +33,7 @@
     sel,
     rows_in,
     prod,
+    relay,
     ret,
     acc,
     pos,
@@ -49,6 +50,11 @@
     sel_recv,
     ret_send,
     ret_recv,
+    leg_send,
+    leg_recv,
+    last_leg_send,
+    last_leg_recv,
+    relay_send,
 ):
     nz = experts // NX
     steps = nz // 2
@@ -62,8 +68,13 @@
     after = (p + 1) % pipes
     before = (p + pipes - 1) % pipes
 
+    leg = steps // 2
+
     def at(zz, xx):
         return ((zz + nz) % nz) * NX + xx
+
+    def slots(xx):
+        return pl.ds(pl.multiple_of(xx * MOST, MOST), MOST)
 
     ids_copy = pltpu.make_async_copy(ids_hbm, ids_ref, local_sem.at[2])
     ids_copy.start()
@@ -221,8 +232,8 @@
 
     def ret_copy(i, half, j, d, local=False):
         xx = (x + d) % NX
-        src = prod.at[i - 1, pl.ds(pl.multiple_of((xx * 2 + half) * MOST, MOST), MOST)]
-        dst = ret.at[j, pl.ds(pl.multiple_of(x * MOST, MOST), MOST)]
+        src = prod.at[i - 1, half, slots(xx)]
+        dst = ret.at[j, slots(x)]
         if local:
             return pltpu.make_async_copy(src, dst, ret_recv.at[j, x])
         return pltpu.make_async_remote_copy(
@@ -233,6 +244,50 @@
             device_id=(p, at(z - j, xx)),
             device_id_type=MESH,
         )
+
+    def leg_copy(i, half):
+        return pltpu.make_async_remote_copy(
+            src_ref=prod.at[i - 1, half],
+            dst_ref=relay.at[i - 1 - leg, half],
+            send_sem=leg_send.at[i - 1, half],
+            recv_sem=leg_recv.at[i - 1, half],
+            device_id=(p, at(z + (2 * half - 1) * leg, x)),
+            device_id_type=MESH,
+        )
+
+    def last_leg_copy(d):
+        rows = slots((x + d) % NX)
+        return pltpu.make_async_remote_copy(
+            src_ref=prod.at[steps - 1, 1, rows],
+            dst_ref=relay.at[steps - 1 - leg, d % 2, rows],
+            send_sem=last_leg_send.at[d],
+            recv_sem=last_leg_recv.at[d],
+            device_id=(p, at(z + (2 * (d % 2) - 1) * leg, x)),
+            device_id_type=MESH,
+        )
+
+    def relay_copy(i, half, d):
+        xx = (x + d) % NX
+        j = i + half * (nz - 2 * i)
+        return pltpu.make_async_remote_copy(
+            src_ref=relay.at[i - 1 - leg, half, slots(xx)],
+            dst_ref=ret.at[j, slots(x)],
+            send_sem=relay_send.at[i - 1, half, d],
+            recv_sem=ret_recv.at[j, x],
+            device_id=(p, at(z + (2 * half - 1) * (i - leg), xx)),
+            device_id_type=MESH,
+        )
+
+    def pass_on(i):
+        for half in range(2):
+            leg_copy(i, half).wait_recv()
+            for d in range(NX):
+                relay_copy(i, half, d).start()
+
+    def pass_on_last():
+        for d in range(NX):
+            last_leg_copy(d).wait_recv()
+            relay_copy(steps, d % 2, d).start()
 
     def multiply(i):
         for d in range(NX):
@@ -250,16 +305,31 @@
                 preferred_element_type=jnp.float32,
             )
             for c in range(0, 256, LANES):
-                prod[i - 1, :, n + c : n + c + LANES] = (
-                    out[:, c : c + LANES] * gates
-                ).astype(jnp.bfloat16)
-        for half, j in enumerate(pair(i)):
-            for d in range(NX):
-                if half == 0 and d == 0:
-                    pl.when(i == steps)(lambda: ret_copy(i, 0, j, 0, local=True).start())
-                    pl.when(i < steps)(lambda: ret_copy(i, 0, j, 0).start())
-                else:
+                scaled = (out[:, c : c + LANES] * gates).astype(jnp.bfloat16)
+                for xx in range(NX):
+                    for half in range(2):
+                        first = (xx * 2 + half) * MOST
+                        prod[
+                            i - 1, half, xx * MOST : (xx + 1) * MOST, n + c : n + c + LANES
+                        ] = scaled[first : first + MOST]
+
+    def send_back(i):
+        @pl.when(i <= leg)
+        def _():
+            for half, j in enumerate(pair(i)):
+                for d in range(NX):
                     ret_copy(i, half, j, d).start()
+
+        @pl.when(i > leg)
+        def _():
+            for half in range(2):
+                leg_copy(i, half).start()
+
+    def send_back_last():
+        for d in range(NX):
+            last_leg_copy(d).start()
+        for d in range(NX):
+            ret_copy(steps, 0, 0, d, local=d == 0).start()
 
     def step(i, carry):
         for c in range(CHUNKS):
@@ -294,14 +364,26 @@
 
         choose(i)
 
-        @pl.when(i >= 2)
-        def _():
-            multiply(i - 1)
+        @pl.when(i > 3)
+        def _():
+            multiply(i - 3)
+            send_back(i - 3)
+
+        @pl.when(i > leg + 4)
+        def _():
+            pass_on(i - 4)
 
         return carry
 
     lax.fori_loop(1, steps + 1, step, 0)
+    multiply(steps - 2)
+    send_back(steps - 2)
+    multiply(steps - 1)
+    send_back(steps - 1)
     multiply(steps)
+    send_back_last()
+    for i in range(max(leg, steps - 4) + 1, steps):
+        pass_on(i)
     acc[...] = jnp.zeros_like(acc)
 
     def place(i, carry):
@@ -325,7 +407,9 @@
                 )
         return carry
 
-    lax.fori_loop(1, steps + 1, place, 0)
+    lax.fori_loop(1, leg, place, 0)
+    pass_on_last()
+    lax.fori_loop(leg, steps + 1, place, 0)
     out_ref[...] = acc[...].astype(jnp.bfloat16)
 
     def drain(i, carry):
@@ -337,15 +421,28 @@
         ring_table(1, i, table.at[0]).wait_send()
         for xx in range(NX):
             sel_copy(i, xx).wait_send()
-        for half, j in enumerate(pair(i)):
-            for d in range(NX):
-                if half == 0 and d == 0:
-                    pl.when(i < steps)(lambda: ret_copy(i, 0, j, 0).wait_send())
-                else:
+
+        @pl.when(i <= leg)
+        def _():
+            for half, j in enumerate(pair(i)):
+                for d in range(NX):
                     ret_copy(i, half, j, d).wait_send()
+
+        @pl.when((i > leg) & (i < steps))
+        def _():
+            for half in range(2):
+                leg_copy(i, half).wait_send()
+                for d in range(NX):
+                    relay_copy(i, half, d).wait_send()
+
         return carry
 
     lax.fori_loop(1, steps + 1, drain, 0)
+    for d in range(NX):
+        last_leg_copy(d).wait_send()
+        relay_copy(steps, d % 2, d).wait_send()
+        if d > 0:
+            ret_copy(steps, 0, 0, d).wait_send()
 
 
 def per_device(pipes, experts, upstream, expert_ids, gate_weights, expert_weight):
@@ -372,7 +469,8 @@
             pltpu.VMEM((MOST, LANES), jnp.bfloat16),
             pltpu.VMEM((steps, NX, 2 * MOST, width + LANES), jnp.bfloat16),
             pltpu.VMEM((steps, NX, 2 * MOST, width + LANES), jnp.bfloat16),
-            pltpu.VMEM((steps, NX * 2 * MOST, hidden), jnp.bfloat16),
+            pltpu.VMEM((steps, 2, NX * MOST, hidden), jnp.bfloat16),
+            pltpu.VMEM((steps // 2, 2, NX * MOST, hidden), jnp.bfloat16),
             pltpu.VMEM((nz, NX * MOST, hidden), jnp.bfloat16),
             pltpu.VMEM((routes, hidden), jnp.float32),
             pltpu.VMEM((routes, LANES), jnp.float32),
@@ -389,6 +487,11 @@
             dma((steps, NX)),
             dma((steps, 2, NX)),
             dma((nz, NX)),
+            dma((steps, 2)),
+            dma((steps, 2)),
+            dma((NX,)),
+            dma((NX,)),
+            dma((steps, 2, NX)),
         ],
         compiler_params=pltpu.CompilerParams(
             collective_id=0, has_side_effects=True, vmem_limit_bytes=62 * 1024 * 1024

time: 144 us -> 134 us (0.931)
  the two profiles are of different devices: /device:TPU:8 before, /device:TPU:24 now
where the time goes in v3:
time: 134 us; the launch traced here: 131 us
  Pallas kernels  129 us (96%)
  local copies, waits for them, and re-layouts  2.06 us (2%)
    pallas_call x1, Pallas kernels, per_device(): pl.pallas_call(functools.partial(kernel, pipes, experts), out_shape=jax.S...  129 us

profile of v3, /device:TPU:24, one launch (start us, length us, event | category | flops | bytes accessed | tf_op | source)
XLA Modules:
  0.0 131.4 jit_solution(14817575228098005739)
XLA Ops:
  0.0 129.4 %shard_map.46 = bf16[512,768]{1,0:T(8,128)(2,1)} custom-call(bf16[64,2048]{1,0:T(8,128)(2,1)} %bitcast.11, s32[8,64]{1,0:T(8,128)} %bitcast.12, bf16[8,64]{1,0:T(8,128)(2,1)} %bitcast.13, bf16[768,2048]{1,0:T(8,128)(2,1)} %bitcast.10), custom_call_target="tpu_custom_call" | custom-call | flops 3221225472 | bytes 8388608 | tf_op jit(solution)/shard_map/pallas_call | solution.py:456
  129.4 2.1 %copy.6 = bf16[1,64,8,768]{3,2,1,0:T(8,128)(2,1)} copy(bf16[1,64,8,768]{3,2,1,0:T(8,128)(2,1)} %bitcast.9) | data formatting | bytes 1572864

commit v4 on v3

--- a/solution.py
+++ b/solution.py
@@ -24,7 +24,7 @@
     experts,
     up_ref,
     ids_hbm,
-    gates_hbm,
+    gates_ref,
     w_hbm,
     out_ref,
     tok,
@@ -39,7 +39,6 @@
     pos,
     w_ref,
     ids_ref,
-    gates_ref,
     local_sem,
     ring_send,
     ring_recv,
@@ -50,9 +49,7 @@
     sel_recv,
     ret_send,
     ret_recv,
-    leg_send,
     leg_recv,
-    last_leg_send,
     last_leg_recv,
     relay_send,
 ):
@@ -73,17 +70,11 @@
     def at(zz, xx):
         return ((zz + nz) % nz) * NX + xx
 
+    def await_all(ref, sem):
+        pltpu.make_async_copy(ref, ref, sem).wait()
+
     def slots(xx):
         return pl.ds(pl.multiple_of(xx * MOST, MOST), MOST)
-
-    ids_copy = pltpu.make_async_copy(ids_hbm, ids_ref, local_sem.at[2])
-    ids_copy.start()
-    gates_copy = pltpu.make_async_copy(gates_hbm, gates_ref, local_sem.at[3])
-    gates_copy.start()
-    own_copy = pltpu.make_async_copy(up_ref, tok.at[0], local_sem.at[0])
-    own_copy.start()
-    w_copy = pltpu.make_async_copy(w_hbm, w_ref, local_sem.at[1])
-    w_copy.start()
 
     barrier = pltpu.get_barrier_semaphore()
 
@@ -92,6 +83,12 @@
     for xx in range(NX):
         pl.semaphore_signal(barrier, inc=1, device_id=(after, at(z, xx)), device_id_type=MESH)
     pl.semaphore_signal(barrier, inc=1, device_id=(before, e), device_id_type=MESH)
+    ids_copy = pltpu.make_async_copy(ids_hbm, ids_ref, local_sem.at[2])
+    ids_copy.start()
+    own_copy = pltpu.make_async_copy(up_ref, tok.at[0], local_sem.at[0])
+    own_copy.start()
+    w_copy = pltpu.make_async_copy(w_hbm, w_ref, local_sem.at[1])
+    w_copy.start()
     pl.semaphore_wait(barrier, 2 + NX + 1)
 
     def ring(direction, hop, src, c):
@@ -100,8 +97,8 @@
         return pltpu.make_async_remote_copy(
             src_ref=src.at[part],
             dst_ref=tok.at[dst, part],
-            send_sem=ring_send.at[direction, hop, c],
-            recv_sem=ring_recv.at[direction, hop, c],
+            send_sem=ring_send.at[0],
+            recv_sem=ring_recv.at[direction, hop - 1, c],
             device_id=(p, at(z + 1 - 2 * direction, x)),
             device_id_type=MESH,
         )
@@ -111,8 +108,8 @@
         return pltpu.make_async_remote_copy(
             src_ref=src,
             dst_ref=table.at[dst],
-            send_sem=table_send.at[direction, hop],
-            recv_sem=table_recv.at[direction, hop],
+            send_sem=table_send.at[0],
+            recv_sem=table_recv.at[direction, hop - 1],
             device_id=(p, at(z + 1 - 2 * direction, x)),
             device_id_type=MESH,
         )
@@ -121,7 +118,6 @@
         for way in range(2):
             ring(way, 1, up_ref, c).start()
     ids_copy.wait()
-    gates_copy.wait()
 
     packed = jnp.concatenate(
         [ids_ref[...].astype(jnp.float32), gates_ref[...].astype(jnp.float32)], axis=0
@@ -193,8 +189,8 @@
         return pltpu.make_async_remote_copy(
             src_ref=sel.at[i - 1, xx],
             dst_ref=rows_in.at[i - 1, x],
-            send_sem=sel_send.at[i - 1, xx],
-            recv_sem=sel_recv.at[i - 1, x],
+            send_sem=sel_send.at[0],
+            recv_sem=sel_recv.at[i - 1],
             device_id=(before, at(z, xx)),
             device_id_type=MESH,
         )
@@ -230,17 +226,17 @@
         for d in range(NX):
             sel_copy(i, (x + d) % NX).start()
 
-    def ret_copy(i, half, j, d, local=False):
+    def ret_copy(i, half, j, d, last=False, local=False):
         xx = (x + d) % NX
         src = prod.at[i - 1, half, slots(xx)]
         dst = ret.at[j, slots(x)]
         if local:
-            return pltpu.make_async_copy(src, dst, ret_recv.at[j, x])
+            return pltpu.make_async_copy(src, dst, ret_recv.at[j])
         return pltpu.make_async_remote_copy(
             src_ref=src,
             dst_ref=dst,
-            send_sem=ret_send.at[i - 1, half, d],
-            recv_sem=ret_recv.at[j, x],
+            send_sem=ret_send.at[1 if last else 0],
+            recv_sem=ret_recv.at[j],
             device_id=(p, at(z - j, xx)),
             device_id_type=MESH,
         )
@@ -249,8 +245,8 @@
         return pltpu.make_async_remote_copy(
             src_ref=prod.at[i - 1, half],
             dst_ref=relay.at[i - 1 - leg, half],
-            send_sem=leg_send.at[i - 1, half],
-            recv_sem=leg_recv.at[i - 1, half],
+            send_sem=ret_send.at[0],
+            recv_sem=leg_recv.at[i - 1 - leg, half],
             device_id=(p, at(z + (2 * half - 1) * leg, x)),
             device_id_type=MESH,
         )
@@ -260,20 +256,20 @@
         return pltpu.make_async_remote_copy(
             src_ref=prod.at[steps - 1, 1, rows],
             dst_ref=relay.at[steps - 1 - leg, d % 2, rows],
-            send_sem=last_leg_send.at[d],
+            send_sem=ret_send.at[2],
             recv_sem=last_leg_recv.at[d],
             device_id=(p, at(z + (2 * (d % 2) - 1) * leg, x)),
             device_id_type=MESH,
         )
 
-    def relay_copy(i, half, d):
+    def relay_copy(i, half, d, last=False):
         xx = (x + d) % NX
         j = i + half * (nz - 2 * i)
         return pltpu.make_async_remote_copy(
             src_ref=relay.at[i - 1 - leg, half, slots(xx)],
             dst_ref=ret.at[j, slots(x)],
-            send_sem=relay_send.at[i - 1, half, d],
-            recv_sem=ret_recv.at[j, x],
+            send_sem=relay_send.at[1 if last else 0],
+            recv_sem=ret_recv.at[j],
             device_id=(p, at(z + (2 * half - 1) * (i - leg), xx)),
             device_id_type=MESH,
         )
@@ -287,14 +283,10 @@
     def pass_on_last():
         for d in range(NX):
             last_leg_copy(d).wait_recv()
-            relay_copy(steps, d % 2, d).start()
+            relay_copy(steps, d % 2, d, last=True).start()
 
     def multiply(i):
-        for d in range(NX):
-            xx = (x + d) % NX
-            pltpu.make_async_copy(
-                rows_in.at[i - 1, xx], rows_in.at[i - 1, xx], sel_recv.at[i - 1, xx]
-            ).wait()
+        await_all(rows_in.at[i - 1], sel_recv.at[i - 1])
         count = NX * 2 * MOST
         gates = rows_in[i - 1, :, :, width:].reshape(count, LANES).astype(jnp.float32)
         for n in range(0, hidden, 256):
@@ -329,7 +321,7 @@
         for d in range(NX):
             last_leg_copy(d).start()
         for d in range(NX):
-            ret_copy(steps, 0, 0, d, local=d == 0).start()
+            ret_copy(steps, 0, 0, d, last=True, local=d == 0).start()
 
     def step(i, carry):
         for c in range(CHUNKS):
@@ -369,29 +361,22 @@
             multiply(i - 3)
             send_back(i - 3)
 
-        @pl.when(i > leg + 4)
-        def _():
-            pass_on(i - 4)
-
         return carry
 
     lax.fori_loop(1, steps + 1, step, 0)
-    multiply(steps - 2)
-    send_back(steps - 2)
-    multiply(steps - 1)
-    send_back(steps - 1)
+    for i in (steps - 2, steps - 1):
+        multiply(i)
+        send_back(i)
     multiply(steps)
     send_back_last()
-    for i in range(max(leg, steps - 4) + 1, steps):
+    for i in range(leg + 1, steps):
         pass_on(i)
     acc[...] = jnp.zeros_like(acc)
 
     def place(i, carry):
         a, b = pair(i)
         for j in (a, b):
-            for xx in range(NX):
-                here = ret.at[j, xx * MOST : (xx + 1) * MOST]
-                pltpu.make_async_copy(here, here, ret_recv.at[j, xx]).wait()
+            await_all(ret.at[j], ret_recv.at[j])
         span = NX * MOST
         part = min(128, routes)
         lane_q = iota((part, 2 * span), 1)
@@ -409,40 +394,19 @@
 
     lax.fori_loop(1, leg, place, 0)
     pass_on_last()
+
+    await_all(tok.at[pl.ds(0, nz - 1)], ring_send.at[0])
+    await_all(table.at[pl.ds(0, nz - 1)], table_send.at[0])
+    await_all(sel, sel_send.at[0])
+    await_all(prod.at[pl.ds(0, steps - 1)], ret_send.at[0])
+    await_all(prod.at[steps - 1, 0, pl.ds(0, (NX - 1) * MOST)], ret_send.at[1])
+    await_all(prod.at[steps - 1, 1], ret_send.at[2])
+    if steps - 1 > leg:
+        await_all(relay.at[pl.ds(0, steps - 1 - leg)], relay_send.at[0])
+    await_all(relay.at[steps - 1 - leg, 0], relay_send.at[1])
+
     lax.fori_loop(leg, steps + 1, place, 0)
     out_ref[...] = acc[...].astype(jnp.bfloat16)
-
-    def drain(i, carry):
-        for c in range(CHUNKS):
-            for way in range(2):
-                last = steps - 1 + (c * 2 // CHUNKS == way)
-                pl.when(i <= last)(lambda: ring(way, i, up_ref, c).wait_send())
-        pl.when(i < steps)(lambda: ring_table(0, i, table.at[0]).wait_send())
-        ring_table(1, i, table.at[0]).wait_send()
-        for xx in range(NX):
-            sel_copy(i, xx).wait_send()
-
-        @pl.when(i <= leg)
-        def _():
-            for half, j in enumerate(pair(i)):
-                for d in range(NX):
-                    ret_copy(i, half, j, d).wait_send()
-
-        @pl.when((i > leg) & (i < steps))
-        def _():
-            for half in range(2):
-                leg_copy(i, half).wait_send()
-                for d in range(NX):
-                    relay_copy(i, half, d).wait_send()
-
-        return carry
-
-    lax.fori_loop(1, steps + 1, drain, 0)
-    for d in range(NX):
-        last_leg_copy(d).wait_send()
-        relay_copy(steps, d % 2, d).wait_send()
-        if d > 0:
-            ret_copy(steps, 0, 0, d).wait_send()
 
 
 def per_device(pipes, experts, upstream, expert_ids, gate_weights, expert_weight):
@@ -459,7 +423,7 @@
         in_specs=[
             pl.BlockSpec(memory_space=pltpu.HBM),
             pl.BlockSpec(memory_space=pltpu.HBM),
-            pl.BlockSpec(memory_space=pltpu.HBM),
+            pl.BlockSpec(memory_space=pltpu.VMEM),
             pl.BlockSpec(memory_space=pltpu.HBM),
         ],
         out_specs=pl.BlockSpec(memory_space=pltpu.VMEM),
@@ -476,34 +440,31 @@
             pltpu.VMEM((routes, LANES), jnp.float32),
             pltpu.VMEM((hidden, width), jnp.bfloat16),
             pltpu.VMEM((topk, tokens), jnp.int32),
-            pltpu.VMEM((topk, tokens), jnp.bfloat16),
-            dma((4,)),
-            dma((2, steps + 1, CHUNKS)),
-            dma((2, steps + 1, CHUNKS)),
-            dma((2, steps + 1)),
-            dma((2, steps + 1)),
+            dma((3,)),
+            dma((1,)),
+            dma((2, steps, CHUNKS)),
+            dma((1,)),
+            dma((2, steps)),
             dma((2,)),
-            dma((steps, NX)),
-            dma((steps, NX)),
-            dma((steps, 2, NX)),
-            dma((nz, NX)),
-            dma((steps, 2)),
-            dma((steps, 2)),
+            dma((1,)),
+            dma((steps,)),
+            dma((3,)),
+            dma((nz,)),
+            dma((max(1, steps - 1 - steps // 2), 2)),
             dma((NX,)),
-            dma((NX,)),
-            dma((steps, 2, NX)),
+            dma((2,)),
         ],
         compiler_params=pltpu.CompilerParams(
-            collective_id=0, has_side_effects=True, vmem_limit_bytes=62 * 1024 * 1024
+            collective_id=0, has_side_effects=True, vmem_limit_bytes=44 * 1024 * 1024
         ),
         cost_estimate=pl.CostEstimate(
             flops=2 * 2 * routes * width * hidden, bytes_accessed=8 << 20, transcendentals=0
         ),
     )(
-        upstream[0],
-        jnp.swapaxes(expert_ids[0], 0, 1),
+        pltpu.with_memory_space_constraint(upstream[0], pltpu.HBM),
+        pltpu.with_memory_space_constraint(jnp.swapaxes(expert_ids[0], 0, 1), pltpu.HBM),
         jnp.swapaxes(gate_weights[0], 0, 1),
-        expert_weight[0, 0],
+        pltpu.with_memory_space_constraint(expert_weight[0, 0], pltpu.HBM),
     )
     return out.reshape(1, tokens, topk, hidden)
 

time: 134 us -> 129 us (0.963)
  Pallas kernels: 129 us -> 125 us
    pallas_call x1, Pallas kernels: 129 us -> 125 us  [per_device(): pl.pallas_call(functools.partial(kernel, pipes, experts), out_shape=jax.S...]
where the time goes in v4:
time: 129 us; the launch traced here: 127 us
  Pallas kernels  125 us (97%)
  local copies, waits for them, and re-layouts  1.56 us (1%)
    pallas_call x1, Pallas kernels, per_device(): pl.pallas_call(functools.partial(kernel, pipes, experts), out_shape=jax.S...  125 us

profile of v4, /device:TPU:24, one launch (start us, length us, event | category | flops | bytes accessed | tf_op | source)
XLA Modules:
  0.0 127.0 jit_solution(12265227250601698192)
XLA Ops:
  0.0 0.0 copy-start
  0.0 0.7 copy-done
  0.7 125.4 %shard_map.46 = bf16[512,768]{1,0:T(8,128)(2,1)S(1)} custom-call(bf16[64,2048]{1,0:T(8,128)(2,1)} %bitcast.12, s32[8,64]{1,0:T(8,128)} %bitcast.13, bf16[8,64]{1,0:T(8,128)(2,1)S(1)} %bitcast.10, bf16[768,2048]{1,0:T(8,128)(2,1)} %bitcast.11), custom_call_target="tpu_custom_call" | custom-call | flops 3221225472 | bytes 8388608 | tf_op jit(solution)/shard_map/pallas_call | solution.py:420
  126.1 0.9 copy.6
Async XLA Ops:
  0.0 0.7 copy-start

commit v5 on v4

--- a/solution.py
+++ b/solution.py
@@ -154,29 +154,6 @@
     )
     shift.start()
 
-    ranks = []
-    for k in range(topk):
-        hit = (columns[:, k : k + 1] == lane_expert) & (lane < HALF)
-        ranks.append(jnp.sum(jnp.where(hit, rank, 0.0), axis=1, keepdims=True))
-    lane8 = iota((tokens, 2 * topk), 1)
-    both = jnp.where(lane8 < topk, columns, 0.0)
-    for k in range(topk):
-        both = jnp.where(lane8 == topk + k, ranks[k], both)
-    routes = tokens * topk
-    spread = (iota((routes, tokens), 0) // topk == iota((routes, tokens), 1)).astype(jnp.bfloat16)
-    by_route = jnp.dot(spread, both.astype(jnp.bfloat16), preferred_element_type=jnp.float32)
-    which = iota((routes, 2 * topk), 0) % topk
-    lane_r = iota((routes, 2 * topk), 1)
-    slot = jnp.sum(
-        jnp.where(lane_r == which, by_route * MOST, 0.0)
-        + jnp.where(lane_r == which + topk, by_route, 0.0),
-        axis=1,
-        keepdims=True,
-    )
-    slot = slot - (z * (NX * MOST)).astype(jnp.float32)
-    slot = jnp.where(slot < 0.0, slot + float(experts * MOST), slot)
-    pos[...] = jnp.broadcast_to(slot, (routes, LANES))
-
     shift.wait()
     ring_table(0, 1, table.at[0]).start()
     ring_table(1, 1, table.at[0]).start()
@@ -195,34 +172,38 @@
             device_id_type=MESH,
         )
 
-    def choose(i):
+    def pick_rows(i, half, j):
         table_lane = iota((MOST, LANES), 1)
         token_lane = (iota((MOST, tokens), 1) + 1).astype(jnp.float32)
-        for half, j in enumerate(pair(i)):
-            slots = table[j].astype(jnp.float32)
-            picks = []
+        slots = table[j].astype(jnp.float32)
+        picks = []
+        for xx in range(NX):
+            expert = at(z, xx)
+            token = jnp.sum(
+                jnp.where(table_lane == expert, slots, 0.0), axis=1, keepdims=True
+            )
+            weight = jnp.sum(
+                jnp.where(table_lane == expert + HALF, slots, 0.0), axis=1, keepdims=True
+            )
+            picks.append((token == token_lane).astype(jnp.bfloat16))
+            sel[i - 1, xx, half * MOST : (half + 1) * MOST, width:] = jnp.broadcast_to(
+                weight, (MOST, LANES)
+            ).astype(jnp.bfloat16)
+        pick = jnp.concatenate(picks, axis=0)
+        part = min(512, width)
+        for c in range(0, width, part):
+            rows = jnp.dot(
+                pick, tok[j, :, c : c + part], preferred_element_type=jnp.float32
+            ).astype(jnp.bfloat16)
             for xx in range(NX):
-                expert = at(z, xx)
-                token = jnp.sum(
-                    jnp.where(table_lane == expert, slots, 0.0), axis=1, keepdims=True
-                )
-                weight = jnp.sum(
-                    jnp.where(table_lane == expert + HALF, slots, 0.0), axis=1, keepdims=True
-                )
-                picks.append((token == token_lane).astype(jnp.bfloat16))
-                sel[i - 1, xx, half * MOST : (half + 1) * MOST, width:] = jnp.broadcast_to(
-                    weight, (MOST, LANES)
-                ).astype(jnp.bfloat16)
-            pick = jnp.concatenate(picks, axis=0)
-            part = min(512, width)
-            for c in range(0, width, part):
-                rows = jnp.dot(
-                    pick, tok[j, :, c : c + part], preferred_element_type=jnp.float32
-                ).astype(jnp.bfloat16)
-                for xx in range(NX):
-                    sel[i - 1, xx, half * MOST : (half + 1) * MOST, c : c + part] = rows[
-                        xx * MOST : (xx + 1) * MOST
-                    ]
+                sel[i - 1, xx, half * MOST : (half + 1) * MOST, c : c + part] = rows[
+                    xx * MOST : (xx + 1) * MOST
+                ]
+
+    def choose(i):
+        own, other = pair(i)
+        pl.when(i < steps)(lambda: pick_rows(i, 0, own))
+        pick_rows(i, 1, other)
         for d in range(NX):
             sel_copy(i, (x + d) % NX).start()
 
@@ -323,6 +304,9 @@
         for d in range(NX):
             ret_copy(steps, 0, 0, d, last=True, local=d == 0).start()
 
+    own_copy.wait()
+    pick_rows(steps, 0, 0)
+
     def step(i, carry):
         for c in range(CHUNKS):
             for way in range(2):
@@ -349,10 +333,6 @@
         @pl.when(i < steps)
         def _():
             ring_table(1, i + 1, table.at[nz - i]).start()
-
-        @pl.when(i == steps)
-        def _():
-            own_copy.wait()
 
         choose(i)
 
@@ -371,9 +351,32 @@
     send_back_last()
     for i in range(leg + 1, steps):
         pass_on(i)
+    ranks = []
+    for k in range(topk):
+        hit = (columns[:, k : k + 1] == lane_expert) & (lane < HALF)
+        ranks.append(jnp.sum(jnp.where(hit, rank, 0.0), axis=1, keepdims=True))
+    lane8 = iota((tokens, 2 * topk), 1)
+    both = jnp.where(lane8 < topk, columns, 0.0)
+    for k in range(topk):
+        both = jnp.where(lane8 == topk + k, ranks[k], both)
+    routes = tokens * topk
+    spread = (iota((routes, tokens), 0) // topk == iota((routes, tokens), 1)).astype(jnp.bfloat16)
+    by_route = jnp.dot(spread, both.astype(jnp.bfloat16), preferred_element_type=jnp.float32)
+    which = iota((routes, 2 * topk), 0) % topk
+    lane_r = iota((routes, 2 * topk), 1)
+    slot = jnp.sum(
+        jnp.where(lane_r == which, by_route * MOST, 0.0)
+        + jnp.where(lane_r == which + topk, by_route, 0.0),
+        axis=1,
+        keepdims=True,
+    )
+    slot = slot - (z * (NX * MOST)).astype(jnp.float32)
+    slot = jnp.where(slot < 0.0, slot + float(experts * MOST), slot)
+    pos[...] = jnp.broadcast_to(slot, (routes, LANES))
+
     acc[...] = jnp.zeros_like(acc)
 
-    def place(i, carry):
+    def place(i, carry, last=False):
         a, b = pair(i)
         for j in (a, b):
             await_all(ret.at[j], ret_recv.at[j])
@@ -387,9 +390,13 @@
         for r in range(0, routes, part):
             pick = (pos[r : r + part, : 2 * span] == want).astype(jnp.bfloat16)
             for n in range(0, hidden, 256):
-                acc[r : r + part, n : n + 256] += jnp.dot(
+                more = acc[r : r + part, n : n + 256] + jnp.dot(
                     pick, rows[:, n : n + 256], preferred_element_type=jnp.float32
                 )
+                if last:
+                    out_ref[r : r + part, n : n + 256] = more.astype(jnp.bfloat16)
+                else:
+                    acc[r : r + part, n : n + 256] = more
         return carry
 
     lax.fori_loop(1, leg, place, 0)
@@ -405,8 +412,8 @@
         await_all(relay.at[pl.ds(0, steps - 1 - leg)], relay_send.at[0])
     await_all(relay.at[steps - 1 - leg, 0], relay_send.at[1])
 
-    lax.fori_loop(leg, steps + 1, place, 0)
-    out_ref[...] = acc[...].astype(jnp.bfloat16)
+    lax.fori_loop(leg, steps, place, 0)
+    place(steps, 0, last=True)
 
 
 def per_device(pipes, experts, upstream, expert_ids, gate_weights, expert_weight):

time: 129 us -> 130 us (level)
  the two profiles are of different devices: /device:TPU:24 before, /device:TPU:2 now
where the time goes in v5:
time: 130 us
  Pallas kernels  128 us (98%)
  local copies, waits for them, and re-layouts  1.56 us (1%)
    pallas_call x1, Pallas kernels, per_device(): pl.pallas_call(functools.partial(kernel, pipes, experts), out_shape=jax.S...  128 us

profile of v5, /device:TPU:2, one launch (start us, length us, event | category | flops | bytes accessed | tf_op | source)
XLA Modules:
  0.0 129.8 jit_solution(4576064020230868342)
XLA Ops:
  0.0 0.0 copy-start
  0.0 0.7 copy-done
  0.7 128.3 %shard_map.46 = bf16[512,768]{1,0:T(8,128)(2,1)S(1)} custom-call(bf16[64,2048]{1,0:T(8,128)(2,1)} %bitcast.12, s32[8,64]{1,0:T(8,128)} %bitcast.13, bf16[8,64]{1,0:T(8,128)(2,1)S(1)} %bitcast.10, bf16[768,2048]{1,0:T(8,128)(2,1)} %bitcast.11), custom_call_target="tpu_custom_call" | custom-call | flops 3221225472 | bytes 8388608 | tf_op jit(solution)/shard_map/pallas_call | solution.py:427
  128.9 0.9 copy.6
Async XLA Ops:
  0.0 0.7 copy-start
